TPU v7x, 256 devices: a whole 4x4x8 slice. The times are simulated.
256 devices in a mesh: px: 8 (over z), py: 32 (over x, y, core).
Axes of the slice: x: 4, y: 4, z: 8, core: 2. Of those that a mesh axis runs over, the one named last changes fastest.
Arguments:
- right_side: float32 [8, 2048, 2048], P(None, 'py', 'px'), may hold values from -6 to 6
- solution_in: float32 [8, 2048, 2048], P(None, 'py', 'px'), may hold values from -4 to 4
- classes: int32 [8, 2048, 2048], P(None, 'py', 'px'), may hold values from 0 to 15
- coeff_table: float32 [16], replicated, may hold values from 0.2 to 5
- eigenvectors: bfloat16 [2048, 2048], replicated, may hold values from -0.053880558 to 0.053880558, as said below
- eigenvalues: float32 [2048], replicated, may hold values from 0.01 to 4
- level_shift: float32 [8], replicated, may hold values from 0.3 to 3
Outputs:
- solution: float32 [8, 2048, 2048], P(None, 'py', 'px')
- residual: float32 [8, 2048, 2048], P(None, 'py', 'px')
- direction: float32 [8, 2048, 2048], P(None, 'py', 'px')
Inputs may be any that keep to these rules, and one draw needn't show every extreme that they name: eigenvectors is a symmetric matrix.
All inputs are finite; a program needn't handle non-finite values.
Results may differ from a plain program's by a relative error of at most 0.034.
Values may be sent and summed in bfloat16 or wider, within the bound.
A program may use at most 64 MiB of HBM per device.

v0:
```python
import jax
import jax.numpy as jnp
from jax import lax
from jax.sharding import PartitionSpec as P

ITERS = 2


def padded_2(array, sides, width):
    for axis, dim in sides:
        size, length = (lax.axis_size(axis), array.shape[dim])
        up = [(i, (i + 1) % size) for i in range(size - 1)]
        down = [(j, i) for i, j in up]
        last = lax.slice_in_dim(array, length - width, length, axis=dim)
        initial = lax.slice_in_dim(array, 0, width, axis=dim)
        before = lax.ppermute(last, axis, up)
        after = lax.ppermute(initial, axis, down)
        array = jnp.concatenate([before, array, after], axis=dim)
    return array


def for_sending(array):

    def short(part):
        return part.astype(jnp.bfloat16) if part.dtype == jnp.float32 else part

    return jax.tree.map(short, array)


def face_sum(padded, coeff_pad):
    values = padded[:, 1:-1, 1:-1]
    coeff = coeff_pad[:, 1:-1, 1:-1]
    height = values.shape[1]
    width = values.shape[2]
    result = jnp.zeros_like(values)
    for shift_y, shift_x in ((0, 1), (2, 1), (1, 0), (1, 2)):
        neighbour = padded[:, shift_y : shift_y + height, shift_x : shift_x + width]
        other = coeff_pad[:, shift_y : shift_y + height, shift_x : shift_x + width]
        result = result + 0.5 * (coeff + other) * (values - neighbour)
    vertical = 0.5 * (coeff[:-1] + coeff[1:]) * (values[:-1] - values[1:])
    zero_layer = jnp.zeros_like(values[:1])
    result = (
        result
        + jnp.concatenate((vertical, zero_layer), 0)
        - jnp.concatenate((zero_layer, vertical), 0)
    )
    return result


def precondition(residual, eigenvectors, eigenvalues, level_shift):
    rounded = residual.astype(jnp.bfloat16)
    levels_here = residual.shape[0] // lax.axis_size("px")
    first = jnp.einsum(
        "kyx,xi->kyi",
        lax.all_to_all(rounded, "px", split_axis=0, concat_axis=2, tiled=True),
        eigenvectors,
        preferred_element_type=jnp.float32,
    ).astype(jnp.bfloat16)
    second = jnp.einsum(
        "kyi,yj->kji",
        lax.all_to_all(first, "py", split_axis=2, concat_axis=1, tiled=True),
        eigenvectors,
        preferred_element_type=jnp.float32,
    )
    spectral_cols = second.shape[2]
    eigen_cols = lax.dynamic_slice_in_dim(
        eigenvalues, lax.axis_index("py") * spectral_cols, spectral_cols, 0
    )
    shift_here = lax.dynamic_slice_in_dim(
        level_shift, lax.axis_index("px") * levels_here, levels_here, 0
    )
    denom = eigenvalues[None, :, None] + eigen_cols[None, None, :] + shift_here[:, None, None]
    scaled = (second / denom).astype(jnp.bfloat16)
    fourth = jnp.einsum(
        "kji,yj->kyi", scaled, eigenvectors, preferred_element_type=jnp.float32
    ).astype(jnp.bfloat16)
    returned = lax.all_to_all(fourth, "py", split_axis=1, concat_axis=2, tiled=True)
    pencil = jnp.einsum("kyi,xi->kyx", returned, eigenvectors, preferred_element_type=jnp.float32)
    return lax.all_to_all(
        pencil.astype(jnp.bfloat16), "px", split_axis=2, concat_axis=0, tiled=True
    ).astype(pencil.dtype)


def shards(right_side, solution_in, classes, coeff_table, eigenvectors, eigenvalues, level_shift):
    coeff = jnp.zeros(classes.shape, jnp.float32)
    for label in range(coeff_table.shape[0]):
        coeff = jnp.where(classes == label, coeff_table[label], coeff)
    stacked = padded_2(
        jnp.stack((solution_in, coeff)).astype(jnp.bfloat16), (("px", 3), ("py", 2)), 1
    ).astype(jnp.float32)
    coeff_pad = stacked[1]
    solution = solution_in
    residual = right_side - face_sum(stacked[0], coeff_pad)
    direction = jnp.zeros_like(residual)
    gamma_prev = jnp.float32(1.0)
    for iteration in range(ITERS):
        precond = precondition(residual, eigenvectors, eigenvalues, level_shift)
        gamma = lax.psum(jnp.sum(residual * precond), ("px", "py"))
        if iteration == 0:
            direction = precond
        else:
            direction = precond + gamma / gamma_prev * direction
        padded = padded_2(for_sending(direction), (("px", 2), ("py", 1)), 1).astype(direction.dtype)
        image = face_sum(padded, coeff_pad)
        alpha = gamma / lax.psum(jnp.sum(direction * image), ("px", "py"))
        solution = solution + alpha * direction
        residual = residual - alpha * image
        gamma_prev = gamma
    return (solution, residual, direction)


def solution(mesh):
    in_specs = (P(None, "py", "px"), P(None, "py", "px"), P(None, "py", "px"), P(), P(), P(), P())
    out_specs = (P(None, "py", "px"), P(None, "py", "px"), P(None, "py", "px"))
    return jax.shard_map(shards, mesh=mesh, in_specs=in_specs, out_specs=out_specs, check_vma=False)
```

profile of v0, /device:TPU:1, one launch (start us, length us, event | category | flops | bytes accessed | tf_op | source)
XLA Modules:
  0.0 568.5 jit_solution(7523217841468684797)
XLA Ops:
  0.6 2.0 fusion.71
  2.6 12.1 %fusion.53 = (bf16[1,8,64,256]{3,1,2,0:T(8,128)(2,1)S(1)}, bf16[1,8,64,256]{3,1,2,0:T(8,128)(2,1)S(1)}) fusion(f32[8,64,256]{2,1,0:T(8,128)} %param.8, bf16[]{:T(256)} %bitcast.16, bf16[]{:T(256)} %bitcast.15, bf16[]{:T(256)} %bitcast.14, bf16[]{:T(256)} %bitcast.13, bf16[]{:T(256)} %bitcast.12, bf16[]{:T(256)} %bitcast.11, bf16[]{:T(256)} %bitcast.10, ...), kind=kLoop, calls=%fused_computation.99 | loop fusion | flops 4194304 | bytes 1572896 | tf_op jit(solution)/shard_map/stack | solution.py:89
  14.8 4.4 collective-permute-start
  19.2 1.3 collective-permute-start.1
  20.5 3.6 collective-permute-done
  24.2 4.2 collective-permute-done.1
  28.4 4.8 collective-permute-start.2
  33.2 2.2 collective-permute-start.3
  35.4 3.1 collective-permute-done.3
  39.7 1.2 fusion.67
  40.9 18.6 %all_to_all.117 = bf16[8,64,256]{2,1,0:T(8,128)(2,1)S(1)} all-to-all(bf16[8,64,256]{2,1,0:T(8,128)(2,1)S(1)} %copy.132), channel_id=1, replica_groups=mesh['px'=8,'py'=32] {'px'}, dimensions={0} | all-to-all | bytes 524288 | tf_op jit(solution)/shard_map/all_to_all | solution.py:55
  59.6 1.6 fusion.4
  62.5 11.5 %reduce = bf16[2048,64]{1,0:T(8,128)(2,1)S(1)} reduce(bf16[2048,1,64]{2,1,0:T(2,128)(2,1)S(1)} %bitcast.188, bf16[]{:T(256)} %broadcast.67), dimensions={1}, to_apply=%bitcast.140.reduce_sub_computation | reduce | bytes 524290
  75.1 9.1 %all-to-all-start.1 = ((bf16[32,2,2048]{2,1,0:T(2,128)(2,1)}), bf16[32,2,2048]{2,1,0:T(2,128)(2,1)S(1)}, u32[]{:S(2)}, u32[]{:S(2)}) async-start(bf16[32,2,2048]{2,1,0:T(2,128)(2,1)} %reshape.79), calls=%async_computation.1 | async-start | bytes 524288 | tf_op jit(solution)/shard_map/all_to_all | solution.py:61
  84.9 8.2 %all-to-all-done.1 = bf16[32,2,2048]{2,1,0:T(2,128)(2,1)S(1)} async-done(((bf16[32,2,2048]{2,1,0:T(2,128)(2,1)}), bf16[32,2,2048]{2,1,0:T(2,128)(2,1)S(1)}, u32[]{:S(2)}, u32[]{:S(2)}) %all-to-all-start.1) | async-done | bytes 262176 | tf_op jit(solution)/shard_map/all_to_all | solution.py:61
  96.5 10.6 %fusion.5 = bf16[1,2048,64]{1,2,0:T(8,128)(2,1)S(1)} fusion(bf16[2048,2048]{1,0:T(8,128)(2,1)} %param.11, bf16[2048,64]{0,1:T(8,128)(2,1)S(1)} %reshape.72, f32[]{:T(128)} %bitcast.25, f32[64]{0:T(128)S(1)} %dynamic_slice.8, f32[2048]{0:T(1024)S(1)} %copy-done.2), kind=kOutput, calls=%fused_computation.13 | convolution fusion | flops 1074397184 | bytes 8921348 | tf_op jit(solution)/shard_map/kji,yj->kyi/dot_general | solution.py:74
  107.8 11.5 %reduce.1 = bf16[2048,64]{1,0:T(8,128)(2,1)S(1)} reduce(bf16[2048,1,64]{2,1,0:T(2,128)(2,1)S(1)} %bitcast.190, bf16[]{:T(256)} %broadcast.67), dimensions={1}, to_apply=%bitcast.142.reduce_sub_computation | reduce | bytes 524290
  119.7 12.6 %all_to_all.118 = bf16[32,2,2048]{2,1,0:T(2,128)(2,1)S(1)} all-to-all(bf16[32,2,2048]{2,1,0:T(2,128)(2,1)S(1)} %reshape.81), channel_id=1, replica_groups=mesh['px'=8,'py'=32] {'py'}, dimensions={0} | all-to-all | bytes 524288 | tf_op jit(solution)/shard_map/all_to_all | solution.py:77
  135.6 6.0 %fusion.6 = bf16[1,64,2048]{2,1,0:T(8,128)(2,1)S(1)} fusion(bf16[64,2048]{1,0:T(8,128)(2,1)S(1)} %reshape.73, bf16[2048,2048]{1,0:T(8,128)(2,1)} %param.11), kind=kOutput, calls=%fused_computation.14 | convolution fusion | flops 537001984 | bytes 8912896 | tf_op jit(solution)/shard_map/kyi,xi->kyx/dot_general | solution.py:78
  142.4 11.5 %reduce.2 = bf16[2048,64]{1,0:T(8,128)(2,1)S(1)} reduce(bf16[2048,1,64]{2,1,0:T(2,128)(2,1)S(1)} %bitcast.191, bf16[]{:T(256)} %broadcast.67), dimensions={1}, to_apply=%bitcast.144.reduce_sub_computation | reduce | bytes 524290
  154.4 14.8 %all_to_all.119 = bf16[8,2,8192]{2,1,0:T(2,128)(2,1)S(1)} all-to-all(bf16[8,2,8192]{2,1,0:T(2,128)(2,1)S(1)} %reshape.83), channel_id=1, replica_groups=mesh['px'=8,'py'=32] {'px'}, dimensions={0} | all-to-all | bytes 524288 | tf_op jit(solution)/shard_map/all_to_all | solution.py:79
  170.6 1.3 collective-permute-start.4
  171.9 1.3 collective-permute-start.5
  173.8 3.8 collective-permute-done.5
  177.7 4.8 collective-permute-start.6
  182.5 2.1 collective-permute-start.7
  184.6 2.8 collective-permute-done.7
  188.3 1.9 fusion.11
  190.1 75.7 %all-reduce.6 = (f32[]{:T(128)}, f32[]{:T(128)}) all-reduce(f32[]{:T(128)} %get-tuple-element.13, f32[]{:T(128)} %get-tuple-element.12), channel_id=1, replica_groups=mesh['px'=8,'py'=32] {'px','py'}, use_global_device_ids=true, to_apply=%region_1.2 | all-reduce | flops 2 | bytes 16 | tf_op jit(solution)/shard_map/psum | solution.py:98
  267.2 14.4 %all_to_all.120 = bf16[8,64,256]{2,1,0:T(8,128)(2,1)S(1)} all-to-all(bf16[8,64,256]{2,1,0:T(8,128)(2,1)S(1)} %copy.143), channel_id=1, replica_groups=mesh['px'=8,'py'=32] {'px'}, dimensions={0} | all-to-all | bytes 524288 | tf_op jit(solution)/shard_map/all_to_all | solution.py:55
  281.7 5.0 fusion.7
  287.4 11.5 %reduce.3 = bf16[2048,64]{1,0:T(8,128)(2,1)S(1)} reduce(bf16[2048,1,64]{2,1,0:T(2,128)(2,1)S(1)} %bitcast.192, bf16[]{:T(256)} %broadcast.67), dimensions={1}, to_apply=%bitcast.146.reduce_sub_computation | reduce | bytes 524290
  299.4 15.9 %all_to_all.121 = bf16[32,2,2048]{2,1,0:T(2,128)(2,1)S(1)} all-to-all(bf16[32,2,2048]{2,1,0:T(2,128)(2,1)S(1)} %reshape.85), channel_id=1, replica_groups=mesh['px'=8,'py'=32] {'py'}, dimensions={0} | all-to-all | bytes 524288 | tf_op jit(solution)/shard_map/all_to_all | solution.py:61
  318.6 10.6 %fusion.8 = bf16[1,2048,64]{1,2,0:T(8,128)(2,1)S(1)} fusion(bf16[2048,2048]{1,0:T(8,128)(2,1)} %param.11, bf16[2048,64]{0,1:T(8,128)(2,1)S(1)} %reshape.75, f32[]{:T(128)} %bitcast.25, f32[64]{0:T(128)S(1)} %dynamic_slice.8, f32[2048]{0:T(1024)S(1)} %copy-done.2), kind=kOutput, calls=%fused_computation.16 | convolution fusion | flops 1074397184 | bytes 8921348 | tf_op jit(solution)/shard_map/kji,yj->kyi/dot_general | solution.py:74
  329.9 11.5 %reduce.4 = bf16[2048,64]{1,0:T(8,128)(2,1)S(1)} reduce(bf16[2048,1,64]{2,1,0:T(2,128)(2,1)S(1)} %bitcast.193, bf16[]{:T(256)} %broadcast.67), dimensions={1}, to_apply=%bitcast.148.reduce_sub_computation | reduce | bytes 524290
  341.8 12.6 %all_to_all.122 = bf16[32,2,2048]{2,1,0:T(2,128)(2,1)S(1)} all-to-all(bf16[32,2,2048]{2,1,0:T(2,128)(2,1)S(1)} %reshape.87), channel_id=1, replica_groups=mesh['px'=8,'py'=32] {'py'}, dimensions={0} | all-to-all | bytes 524288 | tf_op jit(solution)/shard_map/all_to_all | solution.py:77
  357.8 6.0 %fusion.9 = bf16[1,64,2048]{2,1,0:T(8,128)(2,1)S(1)} fusion(bf16[64,2048]{1,0:T(8,128)(2,1)S(1)} %reshape.76, bf16[2048,2048]{1,0:T(8,128)(2,1)} %param.11), kind=kOutput, calls=%fused_computation.17 | convolution fusion | flops 537001984 | bytes 8912896 | tf_op jit(solution)/shard_map/kyi,xi->kyx/dot_general | solution.py:78
  364.6 11.5 %reduce.5 = bf16[2048,64]{1,0:T(8,128)(2,1)S(1)} reduce(bf16[2048,1,64]{2,1,0:T(2,128)(2,1)S(1)} %bitcast.189, bf16[]{:T(256)} %broadcast.67), dimensions={1}, to_apply=%bitcast.150.reduce_sub_computation | reduce | bytes 524290
  376.5 14.8 %all_to_all.123 = bf16[8,2,8192]{2,1,0:T(2,128)(2,1)S(1)} all-to-all(bf16[8,2,8192]{2,1,0:T(2,128)(2,1)S(1)} %reshape.89), channel_id=1, replica_groups=mesh['px'=8,'py'=32] {'px'}, dimensions={0} | all-to-all | bytes 524288 | tf_op jit(solution)/shard_map/all_to_all | solution.py:79
  393.3 73.0 %psum.30 = f32[]{:T(128)} all-reduce(f32[]{:T(128)} %fusion.16), channel_id=1, replica_groups=mesh['px'=8,'py'=32] {'px','py'}, use_global_device_ids=true, to_apply=%region_5.6 | all-reduce | flops 1 | bytes 8 | tf_op jit(solution)/shard_map/psum | solution.py:98
  467.7 3.7 collective-permute-start.8
  471.4 1.3 collective-permute-start.9
  473.6 3.6 collective-permute-done.9
  477.2 4.0 collective-permute-start.10
  481.2 2.1 collective-permute-start.11
  484.3 1.8 collective-permute-done.11
  487.1 1.8 multiply_reduce_fusion
  488.8 75.8 %psum.31 = f32[]{:T(128)} all-reduce(f32[]{:T(128)} %get-tuple-element.16), channel_id=1, replica_groups=mesh['px'=8,'py'=32] {'px','py'}, use_global_device_ids=true, to_apply=%region_7.8 | all-reduce | flops 1 | bytes 8 | tf_op jit(solution)/shard_map/psum | solution.py:105
  (85 shorter events, 33.7 us)
Async XLA Ops:
  0.6 39.0 %copy-start.1 = (f32[8,64,256]{2,1,0:T(8,128)S(1)}, f32[8,64,256]{2,1,0:T(8,128)}, u32[]{:S(2)}) copy-start(f32[8,64,256]{2,1,0:T(8,128)} %param.7) | copy-start | bytes 1572868
  14.8 9.3 %collective-permute-start = (bf16[2,8,64,1]{3,1,2,0:T(8,128)(2,1)S(1)}, bf16[2,8,64,1]{3,1,2,0:T(8,128)(2,1)S(1)}, u32[]{:S(2)}, u32[]{:S(2)}) collective-permute-start(bf16[2,8,64,1]{3,1,2,0:T(8,128)(2,1)S(1)} %get-tuple-element.33), channel_id=1, source_target_pairs={{0,32},{32,64},{64,96},{96,128},{128,160},{160,192},{192,224},{1,3... | collective-permute-start | bytes 6152 | tf_op jit(solution)/shard_map/ppermute | solution.py:16
  19.2 9.1 %collective-permute-start.1 = (bf16[2,8,64,1]{3,1,2,0:T(8,128)(2,1)S(1)}, bf16[2,8,64,1]{3,1,2,0:T(8,128)(2,1)S(1)}, u32[]{:S(2)}, u32[]{:S(2)}) collective-permute-start(bf16[2,8,64,1]{3,1,2,0:T(8,128)(2,1)S(1)} %get-tuple-element.34), channel_id=1, source_target_pairs={{32,0},{64,32},{96,64},{128,96},{160,128},{192,160},{224,192},{33,... | collective-permute-start | bytes 6152 | tf_op jit(solution)/shard_map/ppermute | solution.py:17
  28.4 7.0 %collective-permute-start.2 = (bf16[2,8,1,258]{3,1,2,0:T(8,128)(2,1)S(1)}, bf16[2,8,1,258]{3,1,2,0:T(8,128)(2,1)S(1)}, u32[]{:S(2)}, u32[]{:S(2)}) collective-permute-start(bf16[2,8,1,258]{3,1,2,0:T(8,128)(2,1)S(1)} %get-tuple-element.27), channel_id=1, source_target_pairs={{0,1},{1,2},{2,3},{3,4},{4,5},{5,6},{6,7},{7,8},{8,9},{9,10},{10,1... | collective-permute-start | bytes 24776 | tf_op jit(solution)/shard_map/ppermute | solution.py:16
  33.2 26.4 %slice-start = ((s8[8388608]{0:T(1024)(128)(4,1)}), s8[4194304]{0:T(1024)(128)(4,1)S(1)}, s32[]{:S(2)}) async-start(s8[8388608]{0:T(1024)(128)(4,1)} %bitcast.174), calls=%async_computation.8 | async-start | bytes 8388608
  33.2 5.3 collective-permute-start.3
  39.7 19.9 %slice-start.1 = ((s8[8388608]{0:T(1024)(128)(4,1)}), s8[4194304]{0:T(1024)(128)(4,1)S(1)}, s32[]{:S(2)}) async-start(s8[8388608]{0:T(1024)(128)(4,1)} %bitcast.174), calls=%async_computation.9 | async-start | bytes 8388608
  59.6 24.7 %copy-start.2 = (f32[2048]{0:T(1024)S(1)}, f32[2048]{0:T(1024)}, u32[]{:S(2)}) copy-start(f32[2048]{0:T(1024)} %param.12) | copy-start | bytes 24580
  59.6 24.7 %copy-start.3 = (f32[8]{0:T(128)S(1)}, f32[8]{0:T(128)}, u32[]{:S(2)}) copy-start(f32[8]{0:T(128)} %param.13) | copy-start | bytes 100
  75.1 18.0 %all-to-all-start.1 = ((bf16[32,2,2048]{2,1,0:T(2,128)(2,1)}), bf16[32,2,2048]{2,1,0:T(2,128)(2,1)S(1)}, u32[]{:S(2)}, u32[]{:S(2)}) async-start(bf16[32,2,2048]{2,1,0:T(2,128)(2,1)} %reshape.79), calls=%async_computation.1 | async-start | bytes 524288 | tf_op jit(solution)/shard_map/all_to_all | solution.py:61
  170.6 3.2 collective-permute-start.4
  171.9 5.7 %collective-permute-start.5 = (bf16[8,64,1]{2,0,1:T(8,128)(2,1)S(1)}, bf16[8,64,1]{2,0,1:T(8,128)(2,1)S(1)}, u32[]{:S(2)}, u32[]{:S(2)}) collective-permute-start(bf16[8,64,1]{2,0,1:T(8,128)(2,1)S(1)} %get-tuple-element.38), channel_id=1, source_target_pairs={{32,0},{64,32},{96,64},{128,96},{160,128},{192,160},{224,192},{33,... | collective-permute-start | bytes 3080 | tf_op jit(solution)/shard_map/ppermute | solution.py:17
  177.7 6.9 %collective-permute-start.6 = (bf16[8,1,258]{2,0,1:T(8,128)(2,1)S(1)}, bf16[8,1,258]{2,0,1:T(8,128)(2,1)S(1)}, u32[]{:S(2)}, u32[]{:S(2)}) collective-permute-start(bf16[8,1,258]{2,0,1:T(8,128)(2,1)S(1)} %get-tuple-element.31), channel_id=1, source_target_pairs={{0,1},{1,2},{2,3},{3,4},{4,5},{5,6},{6,7},{7,8},{8,9},{9,10},{10,1... | collective-permute-start | bytes 12392 | tf_op jit(solution)/shard_map/ppermute | solution.py:16
  182.5 4.9 collective-permute-start.7
  467.5 99.5 %copy-start = (f32[8,64,256]{2,1,0:T(8,128)S(1)}, f32[8,64,256]{2,1,0:T(8,128)}, u32[]{:S(2)}) copy-start(f32[8,64,256]{2,1,0:T(8,128)} %param.8) | copy-start | bytes 1572868
  467.7 5.9 %collective-permute-start.8 = (bf16[8,64,1]{2,0,1:T(8,128)(2,1)S(1)}, bf16[8,64,1]{2,0,1:T(8,128)(2,1)S(1)}, u32[]{:S(2)}, u32[]{:S(2)}) collective-permute-start(bf16[8,64,1]{2,0,1:T(8,128)(2,1)S(1)} %get-tuple-element.35), channel_id=1, source_target_pairs={{0,32},{32,64},{64,96},{96,128},{128,160},{160,192},{192,224},{1,3... | collective-permute-start | bytes 3080 | tf_op jit(solution)/shard_map/ppermute | solution.py:16
  471.4 5.7 %collective-permute-start.9 = (bf16[8,64,1]{2,0,1:T(8,128)(2,1)S(1)}, bf16[8,64,1]{2,0,1:T(8,128)(2,1)S(1)}, u32[]{:S(2)}, u32[]{:S(2)}) collective-permute-start(bf16[8,64,1]{2,0,1:T(8,128)(2,1)S(1)} %get-tuple-element.36), channel_id=1, source_target_pairs={{32,0},{64,32},{96,64},{128,96},{160,128},{192,160},{224,192},{33,... | collective-permute-start | bytes 3080 | tf_op jit(solution)/shard_map/ppermute | solution.py:17
  477.2 7.1 %collective-permute-start.10 = (bf16[8,1,258]{2,0,1:T(8,128)(2,1)S(1)}, bf16[8,1,258]{2,0,1:T(8,128)(2,1)S(1)}, u32[]{:S(2)}, u32[]{:S(2)}) collective-permute-start(bf16[8,1,258]{2,0,1:T(8,128)(2,1)S(1)} %get-tuple-element.29), channel_id=1, source_target_pairs={{0,1},{1,2},{2,3},{3,4},{4,5},{5,6},{6,7},{7,8},{8,9},{9,10},{10,1... | collective-permute-start | bytes 12392 | tf_op jit(solution)/shard_map/ppermute | solution.py:16
  481.2 4.9 collective-permute-start.11
where the time goes:
time: 578 us; the launch traced here: 569 us
  blocking collectives  328 us (57%)
  other arithmetic  90.5 us (16%)
  starting transfers between devices  42.4 us (7%)
  matrix products  39.8 us (7%)
  waiting for transfers between devices  32.6 us (6%)
  local copies, waits for them, and re-layouts  29.7 us (5%)
    psum x2, blocking collectives, shards(): gamma = lax.psum(jnp.sum(residual * precond), ('px', 'py'))  149 us
    psum x1, blocking collectives, shards(): alpha = gamma / lax.psum(jnp.sum(direction * image), ('px', 'py'))  75.8 us
    unnamed x7, other arithmetic  69.2 us
    all_to_all x2, blocking collectives, precondition(): lax.all_to_all(rounded, 'px', split_axis=0, concat_axis=2, tiled=True)  33 us
    all_to_all x2, blocking collectives, precondition(): lax.all_to_all(pencil.astype(jnp.bfloat16), 'px', split_axis=2, concat_ax...  29.6 us
    all_to_all x2, blocking collectives, precondition(): lax.all_to_all(fourth, 'py', split_axis=1, concat_axis=2, tiled=True)  25.3 us
    ppermute x6, starting transfers between devices, padded_2(): before = lax.ppermute(last, axis, up)  22.9 us
    dot_general x2, matrix products, precondition(): jnp.einsum('kji,yj->kyi', scaled, eigenvectors, preferred_element_type=jn...  21.1 us
  transfers between devices with their start and end apart: 13, of which 10 were waited for; matrix products, arithmetic and copies ran while one was open for 0% of the time, Pallas kernels for 0%

commit v1 on v0

--- a/solution.py
+++ b/solution.py
@@ -2,6 +2,7 @@
 import jax.numpy as jnp
 from jax import lax
 from jax.sharding import PartitionSpec as P
+from jax.lax import all_to_all, axis_size
 
 ITERS = 2
 
@@ -56,11 +57,11 @@
         eigenvectors,
         preferred_element_type=jnp.float32,
     ).astype(jnp.bfloat16)
+    _handle_sections = lambda tile_in: jnp.concatenate(
+        all_to_all(jnp.stack(jnp.split(tile_in, axis_size("py"), axis=2)), "py", 0, 0), axis=1
+    )
     second = jnp.einsum(
-        "kyi,yj->kji",
-        lax.all_to_all(first, "py", split_axis=2, concat_axis=1, tiled=True),
-        eigenvectors,
-        preferred_element_type=jnp.float32,
+        "kyi,yj->kji", _handle_sections(first), eigenvectors, preferred_element_type=jnp.float32
     )
     spectral_cols = second.shape[2]
     eigen_cols = lax.dynamic_slice_in_dim(

time: 578 us -> 548 us (0.948)
  other arithmetic: 90.5 us -> 67.3 us
    unnamed x7 -> x5, other arithmetic: 69.2 us -> 46.2 us
    unnamed x32 -> x94, local copies, waits for them, and re-layouts: 10.3 us -> 12.8 us
where the time goes in v1:
time: 548 us; the launch traced here: 541 us
  blocking collectives  328 us (60%)
  other arithmetic  67.3 us (12%)
  starting transfers between devices  42.1 us (8%)
  matrix products  39.8 us (7%)
  waiting for transfers between devices  32.6 us (6%)
  local copies, waits for them, and re-layouts  25.6 us (5%)
  between operations  5.67 us (1%)
    psum x2, blocking collectives, shards(): gamma = lax.psum(jnp.sum(residual * precond), ('px', 'py'))  149 us
    psum x1, blocking collectives, shards(): alpha = gamma / lax.psum(jnp.sum(direction * image), ('px', 'py'))  75.8 us
    unnamed x5, other arithmetic  46.2 us
    all_to_all x2, blocking collectives, precondition(): lax.all_to_all(rounded, 'px', split_axis=0, concat_axis=2, tiled=True)  33 us
    all_to_all x2, blocking collectives, precondition(): lax.all_to_all(pencil.astype(jnp.bfloat16), 'px', split_axis=2, concat_ax...  29.6 us
    all_to_all x2, blocking collectives, precondition(): lax.all_to_all(fourth, 'py', split_axis=1, concat_axis=2, tiled=True)  25.5 us
    ppermute x6, starting transfers between devices, padded_2(): before = lax.ppermute(last, axis, up)  22.9 us
    dot_general x2, matrix products, precondition(): jnp.einsum('kji,yj->kyi', scaled, eigenvectors, preferred_element_type=jn...  21.2 us
  transfers between devices with their start and end apart: 13, of which 10 were waited for; matrix products, arithmetic and copies ran while one was open for 0% of the time, Pallas kernels for 0%

profile of v1, /device:TPU:1, one launch (start us, length us, event | category | flops | bytes accessed | tf_op | source)
XLA Modules:
  0.0 541.2 jit_solution(2820518403976896058)
XLA Ops:
  0.6 1.9 fusion.71
  2.6 12.0 %fusion.53 = (bf16[1,8,64,256]{3,1,2,0:T(8,128)(2,1)S(1)}, bf16[1,8,64,256]{3,1,2,0:T(8,128)(2,1)S(1)}) fusion(f32[8,64,256]{2,1,0:T(8,128)} %param.8, bf16[]{:T(256)} %bitcast.16, bf16[]{:T(256)} %bitcast.15, bf16[]{:T(256)} %bitcast.14, bf16[]{:T(256)} %bitcast.13, bf16[]{:T(256)} %bitcast.12, bf16[]{:T(256)} %bitcast.11, bf16[]{:T(256)} %bitcast.10, ...), kind=kLoop, calls=%fused_computation.99 | loop fusion | flops 4194304 | bytes 1572896 | tf_op jit(solution)/shard_map/stack | solution.py:90
  14.8 4.4 collective-permute-start
  19.2 1.3 collective-permute-start.1
  20.5 3.6 collective-permute-done
  24.1 4.2 collective-permute-done.1
  28.4 4.8 collective-permute-start.2
  33.1 2.2 collective-permute-start.3
  35.3 3.1 collective-permute-done.3
  39.6 1.2 fusion.67
  40.9 18.6 %all_to_all.97 = bf16[8,64,256]{2,1,0:T(8,128)(2,1)S(1)} all-to-all(bf16[8,64,256]{2,1,0:T(8,128)(2,1)S(1)} %copy.114), channel_id=1, replica_groups=mesh['px'=8,'py'=32] {'px'}, dimensions={0} | all-to-all | bytes 524288 | tf_op jit(solution)/shard_map/all_to_all | solution.py:56
  59.6 1.6 fusion.4
  62.9 1.1 reshape.81
  64.0 8.9 %all-to-all-start.1 = ((bf16[32,2,2048]{2,1,0:T(2,128)(2,1)}), bf16[32,2,2048]{2,1,0:T(2,128)(2,1)S(1)}, u32[]{:S(2)}, u32[]{:S(2)}) async-start(bf16[32,2,2048]{2,1,0:T(2,128)(2,1)} %reshape.81), calls=%async_computation.1 | async-start | bytes 524288 | tf_op jit(solution)/shard_map/all_to_all | solution.py:61
  73.5 8.2 %all-to-all-done.1 = bf16[32,2,2048]{2,1,0:T(2,128)(2,1)S(1)} async-done(((bf16[32,2,2048]{2,1,0:T(2,128)(2,1)}), bf16[32,2,2048]{2,1,0:T(2,128)(2,1)S(1)}, u32[]{:S(2)}, u32[]{:S(2)}) %all-to-all-start.1) | async-done | bytes 262176 | tf_op jit(solution)/shard_map/all_to_all | solution.py:61
  82.1 10.6 %fusion.5 = bf16[1,2048,64]{1,2,0:T(8,128)(2,1)S(1)} fusion(bf16[2048,2048]{1,0:T(8,128)(2,1)} %param.11, bf16[2048,64]{1,0:T(8,128)(2,1)S(1)} %bitcast.437, f32[]{:T(128)} %bitcast.57, f32[64]{0:T(128)S(1)} %dynamic_slice.8, f32[2048]{0:T(1024)S(1)} %copy-done.2), kind=kOutput, calls=%fused_computation.13 | convolution fusion | flops 1074397184 | bytes 8921348 | tf_op jit(solution)/shard_map/kji,yj->kyi/dot_general | solution.py:75
  93.9 11.5 %reduce = bf16[2048,64]{1,0:T(8,128)(2,1)S(1)} reduce(bf16[2048,1,64]{2,1,0:T(2,128)(2,1)S(1)} %bitcast.430, bf16[]{:T(256)} %broadcast.67), dimensions={1}, to_apply=%bitcast.388.reduce_sub_computation | reduce | bytes 524290
  105.9 12.9 %all_to_all.98 = bf16[32,2,2048]{2,1,0:T(2,128)(2,1)S(1)} all-to-all(bf16[32,2,2048]{2,1,0:T(2,128)(2,1)S(1)} %reshape.83), channel_id=1, replica_groups=mesh['px'=8,'py'=32] {'py'}, dimensions={0} | all-to-all | bytes 524288 | tf_op jit(solution)/shard_map/all_to_all | solution.py:78
  120.5 1.1 copy.118
  122.1 6.0 %fusion.6 = bf16[1,64,2048]{2,1,0:T(8,128)(2,1)S(1)} fusion(bf16[64,2048]{1,0:T(8,128)(2,1)S(1)} %reshape.75, bf16[2048,2048]{1,0:T(8,128)(2,1)} %param.11), kind=kOutput, calls=%fused_computation.14 | convolution fusion | flops 537001984 | bytes 8912896 | tf_op jit(solution)/shard_map/kyi,xi->kyx/dot_general | solution.py:79
  128.8 11.5 %reduce.1 = bf16[2048,64]{1,0:T(8,128)(2,1)S(1)} reduce(bf16[2048,1,64]{2,1,0:T(2,128)(2,1)S(1)} %bitcast.432, bf16[]{:T(256)} %broadcast.67), dimensions={1}, to_apply=%bitcast.390.reduce_sub_computation | reduce | bytes 524290
  140.8 14.8 %all_to_all.99 = bf16[8,2,8192]{2,1,0:T(2,128)(2,1)S(1)} all-to-all(bf16[8,2,8192]{2,1,0:T(2,128)(2,1)S(1)} %reshape.85), channel_id=1, replica_groups=mesh['px'=8,'py'=32] {'px'}, dimensions={0} | all-to-all | bytes 524288 | tf_op jit(solution)/shard_map/all_to_all | solution.py:80
  157.0 1.3 collective-permute-start.4
  158.3 1.3 collective-permute-start.5
  160.2 3.8 collective-permute-done.5
  164.1 4.8 collective-permute-start.6
  168.9 2.1 collective-permute-start.7
  171.0 2.8 collective-permute-done.7
  174.7 1.8 fusion.11
  176.5 75.7 %all-reduce.6 = (f32[]{:T(128)}, f32[]{:T(128)}) all-reduce(f32[]{:T(128)} %get-tuple-element.13, f32[]{:T(128)} %get-tuple-element.12), channel_id=1, replica_groups=mesh['px'=8,'py'=32] {'px','py'}, use_global_device_ids=true, to_apply=%region_1.2 | all-reduce | flops 2 | bytes 16 | tf_op jit(solution)/shard_map/psum | solution.py:99
  253.6 14.4 %all_to_all.100 = bf16[8,64,256]{2,1,0:T(8,128)(2,1)S(1)} all-to-all(bf16[8,64,256]{2,1,0:T(8,128)(2,1)S(1)} %copy.122), channel_id=1, replica_groups=mesh['px'=8,'py'=32] {'px'}, dimensions={0} | all-to-all | bytes 524288 | tf_op jit(solution)/shard_map/all_to_all | solution.py:56
  268.0 5.0 fusion.7
  275.1 15.5 %all_to_all.101 = bf16[32,2,2048]{2,1,0:T(2,128)(2,1)S(1)} all-to-all(bf16[32,2,2048]{2,1,0:T(2,128)(2,1)S(1)} %reshape.87), channel_id=1, replica_groups=mesh['px'=8,'py'=32] {'py'}, dimensions={0} | all-to-all | bytes 524288 | tf_op jit(solution)/shard_map/all_to_all | solution.py:61
  291.0 10.6 %fusion.8 = bf16[1,2048,64]{1,2,0:T(8,128)(2,1)S(1)} fusion(bf16[2048,2048]{1,0:T(8,128)(2,1)} %param.11, bf16[2048,64]{1,0:T(8,128)(2,1)S(1)} %bitcast.436, f32[]{:T(128)} %bitcast.57, f32[64]{0:T(128)S(1)} %dynamic_slice.8, f32[2048]{0:T(1024)S(1)} %copy-done.2), kind=kOutput, calls=%fused_computation.16 | convolution fusion | flops 1074397184 | bytes 8921348 | tf_op jit(solution)/shard_map/kji,yj->kyi/dot_general | solution.py:75
  302.3 11.5 %reduce.2 = bf16[2048,64]{1,0:T(8,128)(2,1)S(1)} reduce(bf16[2048,1,64]{2,1,0:T(2,128)(2,1)S(1)} %bitcast.433, bf16[]{:T(256)} %broadcast.67), dimensions={1}, to_apply=%bitcast.392.reduce_sub_computation | reduce | bytes 524290
  314.2 12.7 %all_to_all.102 = bf16[32,2,2048]{2,1,0:T(2,128)(2,1)S(1)} all-to-all(bf16[32,2,2048]{2,1,0:T(2,128)(2,1)S(1)} %reshape.89), channel_id=1, replica_groups=mesh['px'=8,'py'=32] {'py'}, dimensions={0} | all-to-all | bytes 524288 | tf_op jit(solution)/shard_map/all_to_all | solution.py:78
  330.2 6.0 %fusion.9 = bf16[1,64,2048]{2,1,0:T(8,128)(2,1)S(1)} fusion(bf16[64,2048]{1,0:T(8,128)(2,1)S(1)} %reshape.78, bf16[2048,2048]{1,0:T(8,128)(2,1)} %param.11), kind=kOutput, calls=%fused_computation.17 | convolution fusion | flops 537001984 | bytes 8912896 | tf_op jit(solution)/shard_map/kyi,xi->kyx/dot_general | solution.py:79
  337.0 11.5 %reduce.3 = bf16[2048,64]{1,0:T(8,128)(2,1)S(1)} reduce(bf16[2048,1,64]{2,1,0:T(2,128)(2,1)S(1)} %bitcast.431, bf16[]{:T(256)} %broadcast.67), dimensions={1}, to_apply=%bitcast.394.reduce_sub_computation | reduce | bytes 524290
  349.0 14.8 %all_to_all.103 = bf16[8,2,8192]{2,1,0:T(2,128)(2,1)S(1)} all-to-all(bf16[8,2,8192]{2,1,0:T(2,128)(2,1)S(1)} %reshape.91), channel_id=1, replica_groups=mesh['px'=8,'py'=32] {'px'}, dimensions={0} | all-to-all | bytes 524288 | tf_op jit(solution)/shard_map/all_to_all | solution.py:80
  365.8 73.0 %psum.30 = f32[]{:T(128)} all-reduce(f32[]{:T(128)} %fusion.16), channel_id=1, replica_groups=mesh['px'=8,'py'=32] {'px','py'}, use_global_device_ids=true, to_apply=%region_5.6 | all-reduce | flops 1 | bytes 8 | tf_op jit(solution)/shard_map/psum | solution.py:99
  440.2 3.7 collective-permute-start.8
  443.9 1.3 collective-permute-start.9
  446.0 3.6 collective-permute-done.9
  449.7 4.0 collective-permute-start.10
  453.7 2.2 collective-permute-start.11
  456.8 1.8 collective-permute-done.11
  459.5 1.8 multiply_reduce_fusion
  461.3 75.8 %psum.31 = f32[]{:T(128)} all-reduce(f32[]{:T(128)} %get-tuple-element.16), channel_id=1, replica_groups=mesh['px'=8,'py'=32] {'px','py'}, use_global_device_ids=true, to_apply=%region_7.8 | all-reduce | flops 1 | bytes 8 | tf_op jit(solution)/shard_map/psum | solution.py:106
  (137 shorter events, 27.3 us)
Async XLA Ops:
  0.6 39.0 %copy-start.1 = (f32[8,64,256]{2,1,0:T(8,128)S(1)}, f32[8,64,256]{2,1,0:T(8,128)}, u32[]{:S(2)}) copy-start(f32[8,64,256]{2,1,0:T(8,128)} %param.7) | copy-start | bytes 1572868
  14.8 9.3 %collective-permute-start = (bf16[2,8,64,1]{3,1,2,0:T(8,128)(2,1)S(1)}, bf16[2,8,64,1]{3,1,2,0:T(8,128)(2,1)S(1)}, u32[]{:S(2)}, u32[]{:S(2)}) collective-permute-start(bf16[2,8,64,1]{3,1,2,0:T(8,128)(2,1)S(1)} %get-tuple-element.33), channel_id=1, source_target_pairs={{0,32},{32,64},{64,96},{96,128},{128,160},{160,192},{192,224},{1,3... | collective-permute-start | bytes 6152 | tf_op jit(solution)/shard_map/ppermute | solution.py:17
  19.2 9.1 %collective-permute-start.1 = (bf16[2,8,64,1]{3,1,2,0:T(8,128)(2,1)S(1)}, bf16[2,8,64,1]{3,1,2,0:T(8,128)(2,1)S(1)}, u32[]{:S(2)}, u32[]{:S(2)}) collective-permute-start(bf16[2,8,64,1]{3,1,2,0:T(8,128)(2,1)S(1)} %get-tuple-element.34), channel_id=1, source_target_pairs={{32,0},{64,32},{96,64},{128,96},{160,128},{192,160},{224,192},{33,... | collective-permute-start | bytes 6152 | tf_op jit(solution)/shard_map/ppermute | solution.py:18
  28.4 7.0 %collective-permute-start.2 = (bf16[2,8,1,258]{3,1,2,0:T(8,128)(2,1)S(1)}, bf16[2,8,1,258]{3,1,2,0:T(8,128)(2,1)S(1)}, u32[]{:S(2)}, u32[]{:S(2)}) collective-permute-start(bf16[2,8,1,258]{3,1,2,0:T(8,128)(2,1)S(1)} %get-tuple-element.27), channel_id=1, source_target_pairs={{0,1},{1,2},{2,3},{3,4},{4,5},{5,6},{6,7},{7,8},{8,9},{9,10},{10,1... | collective-permute-start | bytes 24776 | tf_op jit(solution)/shard_map/ppermute | solution.py:17
  33.1 26.4 %slice-start = ((s8[8388608]{0:T(1024)(128)(4,1)}), s8[4194304]{0:T(1024)(128)(4,1)S(1)}, s32[]{:S(2)}) async-start(s8[8388608]{0:T(1024)(128)(4,1)} %bitcast.418), calls=%async_computation.8 | async-start | bytes 8388608
  33.1 5.3 collective-permute-start.3
  39.6 19.9 %slice-start.1 = ((s8[8388608]{0:T(1024)(128)(4,1)}), s8[4194304]{0:T(1024)(128)(4,1)S(1)}, s32[]{:S(2)}) async-start(s8[8388608]{0:T(1024)(128)(4,1)} %bitcast.418), calls=%async_computation.9 | async-start | bytes 8388608
  59.5 13.3 %copy-start.2 = (f32[2048]{0:T(1024)S(1)}, f32[2048]{0:T(1024)}, u32[]{:S(2)}) copy-start(f32[2048]{0:T(1024)} %param.12) | copy-start | bytes 24580
  59.6 13.4 %copy-start.3 = (f32[8]{0:T(128)S(1)}, f32[8]{0:T(128)}, u32[]{:S(2)}) copy-start(f32[8]{0:T(128)} %param.13) | copy-start | bytes 100
  64.0 17.7 %all-to-all-start.1 = ((bf16[32,2,2048]{2,1,0:T(2,128)(2,1)}), bf16[32,2,2048]{2,1,0:T(2,128)(2,1)S(1)}, u32[]{:S(2)}, u32[]{:S(2)}) async-start(bf16[32,2,2048]{2,1,0:T(2,128)(2,1)} %reshape.81), calls=%async_computation.1 | async-start | bytes 524288 | tf_op jit(solution)/shard_map/all_to_all | solution.py:61
  157.0 3.2 collective-permute-start.4
  158.3 5.7 %collective-permute-start.5 = (bf16[8,64,1]{2,0,1:T(8,128)(2,1)S(1)}, bf16[8,64,1]{2,0,1:T(8,128)(2,1)S(1)}, u32[]{:S(2)}, u32[]{:S(2)}) collective-permute-start(bf16[8,64,1]{2,0,1:T(8,128)(2,1)S(1)} %get-tuple-element.38), channel_id=1, source_target_pairs={{32,0},{64,32},{96,64},{128,96},{160,128},{192,160},{224,192},{33,... | collective-permute-start | bytes 3080 | tf_op jit(solution)/shard_map/ppermute | solution.py:18
  164.1 6.9 %collective-permute-start.6 = (bf16[8,1,258]{2,0,1:T(8,128)(2,1)S(1)}, bf16[8,1,258]{2,0,1:T(8,128)(2,1)S(1)}, u32[]{:S(2)}, u32[]{:S(2)}) collective-permute-start(bf16[8,1,258]{2,0,1:T(8,128)(2,1)S(1)} %get-tuple-element.31), channel_id=1, source_target_pairs={{0,1},{1,2},{2,3},{3,4},{4,5},{5,6},{6,7},{7,8},{8,9},{9,10},{10,1... | collective-permute-start | bytes 12392 | tf_op jit(solution)/shard_map/ppermute | solution.py:17
  168.9 4.9 collective-permute-start.7
  440.0 99.5 %copy-start = (f32[8,64,256]{2,1,0:T(8,128)S(1)}, f32[8,64,256]{2,1,0:T(8,128)}, u32[]{:S(2)}) copy-start(f32[8,64,256]{2,1,0:T(8,128)} %param.8) | copy-start | bytes 1572868
  440.2 5.9 %collective-permute-start.8 = (bf16[8,64,1]{2,0,1:T(8,128)(2,1)S(1)}, bf16[8,64,1]{2,0,1:T(8,128)(2,1)S(1)}, u32[]{:S(2)}, u32[]{:S(2)}) collective-permute-start(bf16[8,64,1]{2,0,1:T(8,128)(2,1)S(1)} %get-tuple-element.35), channel_id=1, source_target_pairs={{0,32},{32,64},{64,96},{96,128},{128,160},{160,192},{192,224},{1,3... | collective-permute-start | bytes 3080 | tf_op jit(solution)/shard_map/ppermute | solution.py:17
  443.9 5.7 %collective-permute-start.9 = (bf16[8,64,1]{2,0,1:T(8,128)(2,1)S(1)}, bf16[8,64,1]{2,0,1:T(8,128)(2,1)S(1)}, u32[]{:S(2)}, u32[]{:S(2)}) collective-permute-start(bf16[8,64,1]{2,0,1:T(8,128)(2,1)S(1)} %get-tuple-element.36), channel_id=1, source_target_pairs={{32,0},{64,32},{96,64},{128,96},{160,128},{192,160},{224,192},{33,... | collective-permute-start | bytes 3080 | tf_op jit(solution)/shard_map/ppermute | solution.py:18
  449.7 7.2 %collective-permute-start.10 = (bf16[8,1,258]{2,0,1:T(8,128)(2,1)S(1)}, bf16[8,1,258]{2,0,1:T(8,128)(2,1)S(1)}, u32[]{:S(2)}, u32[]{:S(2)}) collective-permute-start(bf16[8,1,258]{2,0,1:T(8,128)(2,1)S(1)} %get-tuple-element.29), channel_id=1, source_target_pairs={{0,1},{1,2},{2,3},{3,4},{4,5},{5,6},{6,7},{7,8},{8,9},{9,10},{10,1... | collective-permute-start | bytes 12392 | tf_op jit(solution)/shard_map/ppermute | solution.py:17
  453.7 4.9 collective-permute-start.11
